TPU v7x, 512 devices: a whole 4x8x8 slice. The times are simulated.
512 devices in a mesh: grp: 16 (over x_hi, y), dom: 32 (over z, x_lo, core).
Axes of the slice: x: 4 (x_hi: 2, x_lo: 2; x = x_hi * 2 + x_lo), y: 8, z: 8, core: 2. Of those that a mesh axis runs over, the one named last changes fastest.
Arguments:
- particles: float32 [8, 2621440], P(None, ('grp', 'dom')), may hold values from -1.2 to 707, as said below
- ghost_lists: int32 [2, 32768], P(None, ('grp', 'dom')), may hold values from 0 to 1023, as said below
- pair_lists: int32 [4, 393216], P(None, ('grp', 'dom')), may hold values from 1024 to 5119, as said below
Outputs:
- density: float32 [2621440], P(('grp', 'dom'))
- accel: float32 [3, 2621440], P(None, ('grp', 'dom'))
Inputs may be any that keep to these rules, and one draw needn't show every extreme that they name: `particles`: tile t of a domain is its rows t * 64 to (t + 1) * 64 - 1; tiles 0 to 15 are its slab, then four pair regions of 16 tiles. Particles closer than 1 to each other are in the same or adjacent tiles of one domain, or in slab tiles 0 and 15 of domains adjacent along dom in one group, or in tile j of round r's region of partner domains e and e xor k_r and tiles j - 1 to j + 1 of the other. Masses and sound speeds lie in 0.5 to 2. `ghost_lists`: row 0 holds 64 distinct rows of a domain's first 128, row 1 distinct rows of its slab tiles 16 - 2 and 15. `pair_lists`: row r holds, block j after block j, 48 distinct rows of tile j of the domain's r-th pair region.
All inputs are finite; a program needn't handle non-finite values.
Results may differ from a plain program's by a relative error of at most 0.0003.
Values sent between devices are 32-bit elements; how exact they have to be, the bound alone decides.
A program may use at most 64 MiB of HBM per device.

v0:
```python
import jax
import jax.numpy as jnp
from jax import lax
from jax.experimental import pallas as pl
from jax.experimental.pallas import tpu as pltpu
from jax.sharding import PartitionSpec as P

F32 = jnp.float32
REST = 8.0
FAR = -1000.0
LANES = 128
MESH = pl.DeviceIdType.MESH

WALKS = ((0, 4, 0, 4), (10, 8, 8, 16), (28, 8, 24, 32))
SLOTS = 48
FIRST_STEP = (0, 8, 24)
OWN_CHUNKS = 8
LISTED_CHUNKS = 6
OWN_TERMS = 40 * 3 * OWN_CHUNKS
EDGE_TERMS = 6 * OWN_CHUNKS
LISTED_TERMS = 32 * 3 * LISTED_CHUNKS
TERMS = OWN_TERMS + EDGE_TERMS + LISTED_TERMS

ENTRIES = (0, 1, 2, 3, 4, 5, 6, 7, None, 8, 15, 16, 23, 24, 31, 32)
ENTRY = {pair: place for place, pair in enumerate(ENTRIES)}
EDGES = (((None, 3), (4, 8)), ((7, 15), (16, 24)), ((23, 31), (32, None)))


def spread(rows, lanes):
    return lax.gather(
        rows,
        lanes[:, :, None],
        lax.GatherDimensionNumbers(
            offset_dims=(),
            collapsed_slice_dims=(1,),
            start_index_map=(1,),
            operand_batching_dims=(0,),
            start_indices_batching_dims=(0,),
        ),
        slice_sizes=(1, 1),
        mode=lax.GatherScatterMode.PROMISE_IN_BOUNDS,
    )


def total(block):
    return jnp.sum(block, axis=0, keepdims=True)


def kernel(
    particles,
    ghost_lists,
    pair_lists,
    density_out,
    accel_out,
    stack,
    target,
    fields,
    given,
    theirs,
    lists,
    lists_t,
    picks,
    outgoing,
    incoming,
    ghost_out,
    ghost_in,
    dens_out,
    dens_in,
    terms,
    acc_density,
    acc_force,
    row_density,
    row_a,
    row_b,
    row_scale,
    row_member,
    row_force,
    natural,
    extra,
    theirs_given,
    send_sem,
    recv_sem,
):
    grp = lax.axis_index("grp")
    dom = lax.axis_index("dom")
    n_dom = lax.axis_size("dom")

    def flipped(value, bit):
        return value + bit - 2 * bit * (lax.rem(lax.div(value, bit), 2))

    partners = (
        (grp, flipped(dom, 1)),
        (grp, flipped(dom, 4)),
        (flipped(grp, 1), dom),
        (flipped(grp, 2), dom),
    )
    below = (grp, lax.rem(dom + n_dom - 1, n_dom))
    above = (grp, lax.rem(dom + 1, n_dom))

    barrier = pltpu.get_barrier_semaphore()
    for peer in partners + (below, above):
        pl.semaphore_signal(barrier, inc=1, device_id=peer, device_id_type=MESH)

    lane = lax.broadcasted_iota(jnp.int32, (8, LANES), 1)
    first_half = lane < 64
    half = jnp.where(first_half, 0, 1)

    def pick_half(low, high):
        return jnp.where(first_half[0 : low.shape[0]], low, high)

    def swap(block):
        return pltpu.roll(block, 64, 1)

    padded = jnp.concatenate([pair_lists[...], jnp.zeros((4, LANES), jnp.int32)], axis=1)
    padded = jnp.concatenate([padded, padded], axis=0)
    for j in range(16):
        lists[pl.ds(8 * j, 8), :] = jnp.bitwise_and(padded[:, 48 * j : 48 * j + LANES], 63)
    for k in range(8):
        even = lists[pl.ds(16 * k, 8), :]
        odd = lists[pl.ds(16 * k + 8, 8), :]
        both = pick_half(even, swap(odd) + 64)
        for r in range(4):
            picks[pl.ds(8 * r + k, 1), :] = both[r : r + 1]

    for p in range(40):
        stack[pl.ds(8 * p, 8), :] = particles[:, LANES * p : LANES * p + LANES]

    for r in range(4):
        for k in range(8):
            index = jnp.broadcast_to(picks[pl.ds(8 * r + k, 1), :], (8, LANES))
            outgoing[r, pl.ds(8 * k, 8), :] = spread(stack[pl.ds(8 * (8 + 8 * r + k), 8), :], index)
    faces = jnp.concatenate([ghost_lists[...], ghost_lists[...]], axis=1)
    for side, pair in ((0, 0), (1, 7)):
        index = jnp.broadcast_to(jnp.bitwise_and(faces[side : side + 1], 127), (8, LANES))
        ghost_out[side] = spread(stack[pl.ds(8 * pair, 8), :], index)

    pl.semaphore_wait(barrier, 6)

    def send(source, destination, number, peer):
        copy = pltpu.make_async_remote_copy(
            src_ref=source,
            dst_ref=destination,
            send_sem=send_sem.at[number],
            recv_sem=recv_sem.at[number],
            device_id=peer,
            device_id_type=MESH,
        )
        copy.start()
        return copy

    pair_copies = [
        send(outgoing.at[r], incoming.at[pl.ds(64 * r, 64)], r, partners[r]) for r in (3, 2, 1, 0)
    ]
    ghost_copies = [
        send(ghost_out.at[0], ghost_in.at[pl.ds(8, 8)], 4, below),
        send(ghost_out.at[1], ghost_in.at[pl.ds(0, 8)], 5, above),
    ]

    filler_field = lax.broadcasted_iota(jnp.int32, (8, LANES), 0)
    filler = jnp.where(filler_field < 3, FAR, 0.0).astype(F32)
    fields[0] = jnp.transpose(
        jnp.concatenate(
            [filler if pair is None else stack[pl.ds(8 * pair, 8), :] for pair in ENTRIES], axis=0
        )
    )
    fields[1] = jnp.transpose(stack[pl.ds(64, 128), :])
    fields[2] = jnp.transpose(stack[pl.ds(192, 128), :])
    lists_t[...] = jnp.transpose(lists[...].astype(F32))

    zero = jnp.zeros((8, LANES), F32)
    for base, pairs, low, high in WALKS:
        for k in range(pairs):
            one = stack[pl.ds(8 * (low + k), 8), :]
            two = stack[pl.ds(8 * (high + k), 8), :]
            target[pl.ds(8 * (base + 1 + 2 * k), 8), :] = pick_half(one, swap(two))
            target[pl.ds(8 * (base + 2 + 2 * k), 8), :] = pick_half(swap(one), two)
        target[pl.ds(8 * base, 8), :] = zero
        target[pl.ds(8 * (base + 1 + 2 * pairs), 8), :] = zero
    for slot in (46, 47):
        target[pl.ds(8 * slot, 8), :] = zero

    def meet(block, row, lanes, chunks, slots, term):
        sums = [zero for _ in slots]
        aims = [
            [
                jnp.broadcast_to(target[pl.ds(8 * slot + f, 1), :], (8, LANES))
                for f in range(6)
            ]
            for slot in slots
        ]
        for c in range(chunks):
            rows = block[pl.ds(row + 8 * c, 8), :]
            xs, ys, zs, us, vs, ws, mass = [spread(rows, lanes + f) for f in range(7)]
            for n in range(len(slots)):
                xt, yt, zt, ut, vt, wt = aims[n]
                dx, dy, dz = xt - xs, yt - ys, zt - zs
                squared = dx * dx + dy * dy + dz * dz
                near = jnp.maximum(1.0 - squared, 0.0)
                near2 = near * near
                sums[n] = sums[n] + mass * (near2 * near)
                along = (ut - us) * dx + (vt - vs) * dy + (wt - ws) * dz
                place = term + 4 * (c * len(slots) + n)
                terms[place] = along * lax.rsqrt(jnp.maximum(squared, 0.01))
                terms[place + 1] = near2 * dx
                terms[place + 2] = near2 * dy
                terms[place + 3] = near2 * dz
        return sums

    def edge_lanes(pair_low, pair_high, stride, scale):
        return jnp.where(first_half, scale * ENTRY[pair_low], scale * ENTRY[pair_high])

    def own_density(walk):
        base, pairs, low, high = WALKS[walk]
        before, after = EDGES[walk]
        block = fields.at[walk]
        span = half * (32 if walk == 0 else 64)
        edge_term = 4 * (OWN_TERMS + 2 * walk * OWN_CHUNKS)
        (start,) = meet(
            fields.at[0], 64, edge_lanes(*before, 1, 8), OWN_CHUNKS, [base + 1], edge_term
        )

        def step(k, carry):
            waiting, current = carry
            for odd in (0, 1):
                slot = base + 2 * k + odd
                term = 4 * 3 * OWN_CHUNKS * (FIRST_STEP[walk] + 2 * k + odd)
                behind, here, ahead = meet(
                    block, 64 * odd, span + 8 * k, OWN_CHUNKS, [slot, slot + 1, slot + 2], term
                )
                acc_density[slot] = waiting + behind
                waiting, current = current + here, ahead
            return waiting, current

        waiting, _ = lax.fori_loop(0, pairs, step, (zero, start))
        (end,) = meet(
            fields.at[0],
            0,
            edge_lanes(*after, 1, 8),
            OWN_CHUNKS,
            [base + 2 * pairs],
            edge_term + 4 * OWN_CHUNKS,
        )
        acc_density[base + 2 * pairs] = waiting + end

    own_density(1)
    own_density(2)

    place_in_tile = jnp.bitwise_and(lane, 63).astype(F32)

    def listed_density(walk):
        base, pairs, low, high = WALKS[walk]
        block = theirs.at[walk - 1]

        def member(slot, step):
            lanes = 8 * step + 2 * (walk - 1) + half
            found = zero
            for c in range(LISTED_CHUNKS):
                named = spread(lists_t[pl.ds(8 * c, 8), :], lanes)
                found = found + jnp.where(named == place_in_tile, 1.0, 0.0)
            row_member[pl.ds(slot, 1), :] = total(found)

        def finish(slot, added):
            inside = jnp.broadcast_to(row_member[pl.ds(slot, 1), :], (8, LANES))
            row_density[pl.ds(slot, 1), :] = total(acc_density[slot] + inside * added)

        row_member[pl.ds(base, 1), :] = zero[0:1]
        acc_density[base] = zero

        def step(k, carry):
            waiting, current = carry
            for odd in (0, 1):
                slot = base + 2 * k + odd
                member(slot + 1, 2 * k + odd)
                term = 4 * (OWN_TERMS + EDGE_TERMS) + 4 * 3 * LISTED_CHUNKS * (
                    16 * (walk - 1) + 2 * k + odd
                )
                behind, here, ahead = meet(
                    block,
                    64 * odd,
                    64 * half + 8 * k,
                    LISTED_CHUNKS,
                    [slot, slot + 1, slot + 2],
                    term,
                )
                finish(slot, waiting + behind)
                waiting, current = current + here, ahead
            return waiting, current

        waiting, _ = lax.fori_loop(0, pairs, step, (zero, zero))
        finish(base + 2 * pairs, waiting)

    def to_pairs(rows, walk):
        base, pairs, low, high = WALKS[walk]
        even = rows[pl.ds(base + 1, pairs, stride=2), :]
        odd = rows[pl.ds(base + 2, pairs, stride=2), :]
        return pick_half(even, swap(odd)), pick_half(swap(even), odd)

    for copy in pair_copies[2:]:
        copy.wait_recv()
    theirs[0] = jnp.transpose(incoming[pl.ds(0, 128), :])
    listed_density(1)
    for copy in pair_copies[:2]:
        copy.wait_recv()
    theirs[1] = jnp.transpose(incoming[pl.ds(128, 128), :])
    listed_density(2)
    for walk in (1, 2):
        base, pairs, low, high = WALKS[walk]
        one, two = to_pairs(row_density, walk)
        natural[pl.ds(low, 8), :] = one
        natural[pl.ds(high, 8), :] = two
        for r, rows in ((2 * walk - 2, one), (2 * walk - 1, two)):
            dens_out[r] = spread(rows, picks[pl.ds(8 * r, 8), :])
    dens_copies = [
        send(dens_out.at[r], dens_in.at[r], 6 + r, partners[r]) for r in (3, 2, 1, 0)
    ]

    own_density(0)
    for copy in ghost_copies:
        copy.wait_recv()
    ghosts = theirs_given
    ghosts[...] = jnp.transpose(ghost_in[...])

    def ghost_density(pair, side):
        sums = zero
        aims = [
            jnp.broadcast_to(stack[pl.ds(8 * pair + f, 1), :], (8, LANES)) for f in range(3)
        ]
        at = jnp.zeros((8, LANES), jnp.int32) + 8 * side
        for c in range(OWN_CHUNKS):
            rows = ghosts[pl.ds(8 * c, 8), :]
            dx, dy, dz = [aims[f] - spread(rows, at + f) for f in range(3)]
            near = jnp.maximum(1.0 - (dx * dx + dy * dy + dz * dz), 0.0)
            sums = sums + spread(rows, at + 6) * (near * near * near)
        return sums

    from_lower = jnp.where(dom > 0, ghost_density(0, 0), 0.0)
    from_upper = jnp.where(dom < n_dom - 1, ghost_density(7, 1), 0.0)
    acc_density[1] = acc_density[1] + pick_half(from_lower, zero)
    acc_density[2] = acc_density[2] + pick_half(swap(from_lower), zero)
    acc_density[7] = acc_density[7] + pick_half(zero, swap(from_upper))
    acc_density[8] = acc_density[8] + pick_half(zero, from_upper)
    for slot in range(1, 9):
        row_density[pl.ds(slot, 1), :] = total(acc_density[slot])
    one, two = to_pairs(row_density, 0)
    natural[pl.ds(0, 4), :] = one
    natural[pl.ds(4, 4), :] = two
    density_out[...] = natural[...]

    for slot in (0, 9, 10, 27, 28, 45, 46, 47):
        row_density[pl.ds(slot, 1), :] = zero[0:1] + 1.0
    for at in range(0, SLOTS, 8):
        rho = row_density[pl.ds(at, 8), :]
        sound = jnp.maximum(target[pl.ds(8 * at + 7, 8, stride=8), :], 0.5)
        inverse = 1.0 / rho
        row_a[pl.ds(at, 8), :] = sound - REST * sound * inverse
        row_b[pl.ds(at, 8), :] = 1.0 / (rho * sound)
        row_scale[pl.ds(at, 8), :] = 12.0 * inverse

    def values(rho, sound, mass):
        inverse = 1.0 / rho
        return [sound - REST * sound * inverse, 1.0 / (rho * sound), mass * inverse]

    own_values = []
    for at in range(0, 40, 8):
        own_values.append(
            values(
                natural[pl.ds(at, 8), :],
                stack[pl.ds(8 * at + 7, 8, stride=8), :],
                stack[pl.ds(8 * at + 6, 8, stride=8), :],
            )
        )
    blank = jnp.zeros((32, LANES), F32)
    given[1] = jnp.transpose(
        jnp.concatenate([own_values[n][f] for n in (1, 2, 3, 4) for f in range(3)] + [blank], axis=0)
    )
    for f in range(3):
        extra[pl.ds(16 * f, 8), :] = own_values[0][f]
        extra[pl.ds(16 * f + 8, 1), :] = zero[0:1] + (1.0 if f == 1 else 0.0)
        for place in range(9, 16):
            group, within = divmod(ENTRIES[place], 8)
            extra[pl.ds(16 * f + place, 1), :] = own_values[group][f][within : within + 1]
    extra[pl.ds(48, 80), :] = jnp.zeros((80, LANES), F32)
    given[0] = jnp.transpose(extra[...])

    def push(block, row, lanes, field_stride, chunks, slots, term):
        sums = [[zero, zero, zero] for _ in slots]
        aims = [
            [jnp.broadcast_to(rows[pl.ds(slot, 1), :], (8, LANES)) for rows in (row_a, row_b)]
            for slot in slots
        ]
        for c in range(chunks):
            rows = block[pl.ds(row + 8 * c, 8), :]
            a_source, b_source, gain = [spread(rows, lanes + field_stride * f) for f in range(3)]
            for n in range(len(slots)):
                place = term + 4 * (c * len(slots) + n)
                star = (aims[n][0] + a_source) - terms[place]
                factor = star * (1.0 / (aims[n][1] + b_source)) * gain
                for f in range(3):
                    sums[n][f] = sums[n][f] + factor * terms[place + 1 + f]
        return sums

    def plus(one, two):
        return [a + b for a, b in zip(one, two)]

    zeros = [zero, zero, zero]

    def own_force(walk):
        base, pairs, low, high = WALKS[walk]
        before, after = EDGES[walk]
        span = 4 * half if walk == 0 else 24 * half + 48 * (walk - 1)
        block = given.at[0 if walk == 0 else 1]
        field_stride = 16 if walk == 0 else 8
        edge_term = 4 * (OWN_TERMS + 2 * walk * OWN_CHUNKS)
        (start,) = push(
            given.at[0], 64, edge_lanes(*before, 16, 1), 16, OWN_CHUNKS, [base + 1], edge_term
        )

        def keep(slot, sums):
            for f in range(3):
                acc_force[3 * slot + f] = sums[f]

        def step(k, carry):
            waiting, current = carry
            for odd in (0, 1):
                slot = base + 2 * k + odd
                term = 4 * 3 * OWN_CHUNKS * (FIRST_STEP[walk] + 2 * k + odd)
                behind, here, ahead = push(
                    block,
                    64 * odd,
                    span + k,
                    field_stride,
                    OWN_CHUNKS,
                    [slot, slot + 1, slot + 2],
                    term,
                )
                keep(slot, plus(waiting, behind))
                waiting, current = plus(current, here), ahead
            return waiting, current

        waiting, _ = lax.fori_loop(0, pairs, step, (zeros, start))
        (end,) = push(
            given.at[0],
            0,
            edge_lanes(*after, 16, 1),
            16,
            OWN_CHUNKS,
            [base + 2 * pairs],
            edge_term + 4 * OWN_CHUNKS,
        )
        keep(base + 2 * pairs, plus(waiting, end))

    for walk in range(3):
        own_force(walk)

    for copy in dens_copies:
        copy.wait_recv()
    partner_values = []
    for r in range(4):
        for value in values(
            jnp.maximum(dens_in[r], 0.01),
            jnp.maximum(incoming[pl.ds(64 * r + 7, 8, stride=8), :], 0.5),
            incoming[pl.ds(64 * r + 6, 8, stride=8), :],
        ):
            partner_values.append(value)
    theirs_given[...] = jnp.transpose(jnp.concatenate(partner_values + [blank], axis=0))

    def listed_force(walk):
        base, pairs, low, high = WALKS[walk]

        def finish(slot, added):
            inside = jnp.broadcast_to(row_member[pl.ds(slot, 1), :], (8, LANES))
            scale = row_scale[pl.ds(slot, 1), :]
            for f in range(3):
                sums = total(acc_force[3 * slot + f] + inside * added[f])
                row_force[pl.ds(SLOTS * f + slot, 1), :] = sums * scale

        for f in range(3):
            acc_force[3 * base + f] = zero

        def step(k, carry):
            waiting, current = carry
            for odd in (0, 1):
                slot = base + 2 * k + odd
                term = 4 * (OWN_TERMS + EDGE_TERMS) + 4 * 3 * LISTED_CHUNKS * (
                    16 * (walk - 1) + 2 * k + odd
                )
                behind, here, ahead = push(
                    theirs_given,
                    64 * odd,
                    24 * half + (48 * (walk - 1) + k),
                    8,
                    LISTED_CHUNKS,
                    [slot, slot + 1, slot + 2],
                    term,
                )
                finish(slot, plus(waiting, behind))
                waiting, current = plus(current, here), ahead
            return waiting, current

        waiting, _ = lax.fori_loop(0, pairs, step, (zeros, zeros))
        finish(base + 2 * pairs, waiting)

    for slot in range(1, 9):
        for f in range(3):
            row_force[pl.ds(SLOTS * f + slot, 1), :] = (
                total(acc_force[3 * slot + f]) * row_scale[pl.ds(slot, 1), :]
            )
    listed_force(1)
    listed_force(2)
    for f in range(3):
        for walk in range(3):
            base, pairs, low, high = WALKS[walk]
            one, two = to_pairs(row_force.at[pl.ds(SLOTS * f, SLOTS)], walk)
            accel_out[f, pl.ds(low, pairs), :] = one
            accel_out[f, pl.ds(high, pairs), :] = two
    for copy in pair_copies + ghost_copies + dens_copies:
        copy.wait_send()


def local(particles, ghost_lists, pair_lists):
    vmem = pl.BlockSpec(memory_space=pltpu.VMEM)
    density, accel = pl.pallas_call(
        kernel,
        out_shape=(
            jax.ShapeDtypeStruct((40, LANES), F32),
            jax.ShapeDtypeStruct((3, 40, LANES), F32),
        ),
        in_specs=[vmem, vmem, vmem],
        out_specs=(vmem, vmem),
        scratch_shapes=[
            pltpu.VMEM((320, LANES), F32),
            pltpu.VMEM((8 * SLOTS, LANES), F32),
            pltpu.VMEM((3, 128, LANES), F32),
            pltpu.VMEM((2, 128, LANES), F32),
            pltpu.VMEM((2, 128, LANES), F32),
            pltpu.VMEM((128, LANES), jnp.int32),
            pltpu.VMEM((128, LANES), F32),
            pltpu.VMEM((32, LANES), jnp.int32),
            pltpu.VMEM((4, 64, LANES), F32),
            pltpu.VMEM((256, LANES), F32),
            pltpu.VMEM((2, 8, LANES), F32),
            pltpu.VMEM((128, LANES), F32),
            pltpu.VMEM((4, 8, LANES), F32),
            pltpu.VMEM((4, 8, LANES), F32),
            pltpu.VMEM((4 * TERMS, 8, LANES), F32),
            pltpu.VMEM((SLOTS, 8, LANES), F32),
            pltpu.VMEM((3 * SLOTS, 8, LANES), F32),
            pltpu.VMEM((SLOTS, LANES), F32),
            pltpu.VMEM((SLOTS, LANES), F32),
            pltpu.VMEM((SLOTS, LANES), F32),
            pltpu.VMEM((SLOTS, LANES), F32),
            pltpu.VMEM((SLOTS, LANES), F32),
            pltpu.VMEM((3 * SLOTS, LANES), F32),
            pltpu.VMEM((40, LANES), F32),
            pltpu.VMEM((128, LANES), F32),
            pltpu.VMEM((128, LANES), F32),
            pltpu.SemaphoreType.DMA((10,)),
            pltpu.SemaphoreType.DMA((10,)),
        ],
        compiler_params=pltpu.CompilerParams(
            collective_id=0, has_side_effects=True, vmem_limit_bytes=44 * 1024 * 1024
        ),
    )(particles, ghost_lists, pair_lists)
    return density.reshape(-1), accel.reshape(3, -1)


def solution(mesh):
    in_specs = (P(None, ("grp", "dom")), P(None, ("grp", "dom")), P(None, ("grp", "dom")))
    out_specs = (P(("grp", "dom")), P(None, ("grp", "dom")))
    return jax.shard_map(local, mesh=mesh, in_specs=in_specs, out_specs=out_specs, check_vma=False)
```

profile of v0, /device:TPU:56, one launch (start us, length us, event | category | flops | bytes accessed | tf_op | source)
XLA Modules:
  0.0 36.5 jit_solution(1697610266477248200)
XLA Ops:
  0.6 0.0 copy-start
  0.6 0.9 %copy-done = f32[8,5120]{1,0:T(8,128)S(1)} copy-done((f32[8,5120]{1,0:T(8,128)S(1)}, f32[8,5120]{1,0:T(8,128)}, u32[]{:S(2)}) %copy-start) | copy-done | bytes 163864
  1.5 0.0 copy-start.1
  1.5 0.7 %copy-done.1 = s32[4,768]{1,0:T(4,128)S(1)} copy-done((s32[4,768]{1,0:T(4,128)S(1)}, s32[4,768]{1,0:T(4,128)}, u32[]{:S(2)}) %copy-start.1) | copy-done | bytes 12312
  2.3 0.0 copy-start.2
  2.3 0.7 %copy-done.2 = s32[2,64]{1,0:T(2,128)S(1)} copy-done((s32[2,64]{1,0:T(2,128)S(1)}, s32[2,64]{1,0:T(2,128)}, u32[]{:S(2)}) %copy-start.2) | copy-done | bytes 536
  2.9 32.3 %shard_map.50 = (f32[40,128]{1,0:T(8,128)S(1)}, f32[3,40,128]{2,1,0:T(8,128)S(1)}) custom-call(f32[8,5120]{1,0:T(8,128)S(1)} %copy-done, s32[2,64]{1,0:T(2,128)S(1)} %copy-done.2, s32[4,768]{1,0:T(4,128)S(1)} %copy-done.1), custom_call_target="tpu_custom_call" | custom-call | tf_op jit(solution)/shard_map/pallas_call | solution.py:522
  35.2 0.7 %copy.7 = f32[1,3,40,128]{3,1,2,0:T(4,128)} copy(f32[1,3,40,128]{3,2,1,0:T(8,128)S(1)} %bitcast.5) | data formatting | bytes 122880
  35.9 0.6 %copy.9 = f32[5120]{0:T(1024)} copy(f32[5120]{0:T(1024)S(1)} %bitcast.6) | data formatting | bytes 40960
Async XLA Ops:
  0.6 0.9 %copy-start = (f32[8,5120]{1,0:T(8,128)S(1)}, f32[8,5120]{1,0:T(8,128)}, u32[]{:S(2)}) copy-start(f32[8,5120]{1,0:T(8,128)} %particles.1) | copy-start | bytes 491524
  1.5 0.7 %copy-start.1 = (s32[4,768]{1,0:T(4,128)S(1)}, s32[4,768]{1,0:T(4,128)}, u32[]{:S(2)}) copy-start(s32[4,768]{1,0:T(4,128)} %pair_lists.1) | copy-start | bytes 36868
  2.3 0.7 %copy-start.2 = (s32[2,64]{1,0:T(2,128)S(1)}, s32[2,64]{1,0:T(2,128)}, u32[]{:S(2)}) copy-start(s32[2,64]{1,0:T(2,128)} %ghost_lists.1) | copy-start | bytes 1540
where the time goes:
time: 36.7 us; the launch traced here: 36.5 us
  Pallas kernels  32.3 us (88%)
  local copies, waits for them, and re-layouts  3.56 us (10%)
  between operations  0.65 us (2%)
    pallas_call x1, Pallas kernels, local(): pl.pallas_call(kernel, out_shape=(jax.ShapeDtypeStruct((40, LANES), F32),...  32.3 us
    unnamed x8, local copies, waits for them, and re-layouts  3.56 us

commit v1 on v0

--- a/solution.py
+++ b/solution.py
@@ -47,11 +47,15 @@
 
 
 def kernel(
+    particles_hbm,
+    ghost_hbm,
+    lists_hbm,
+    density_out,
+    accel_out,
     particles,
     ghost_lists,
     pair_lists,
-    density_out,
-    accel_out,
+    rings,
     stack,
     target,
     fields,
@@ -78,9 +82,19 @@
     natural,
     extra,
     theirs_given,
+    load_sem,
     send_sem,
     recv_sem,
 ):
+    loads = [
+        pltpu.make_async_copy(source, destination, load_sem.at[number])
+        for number, (source, destination) in enumerate(
+            ((lists_hbm, pair_lists), (particles_hbm, particles), (ghost_hbm, ghost_lists))
+        )
+    ]
+    for load in loads:
+        load.start()
+
     grp = lax.axis_index("grp")
     dom = lax.axis_index("dom")
     n_dom = lax.axis_size("dom")
@@ -111,6 +125,7 @@
     def swap(block):
         return pltpu.roll(block, 64, 1)
 
+    loads[0].wait()
     padded = jnp.concatenate([pair_lists[...], jnp.zeros((4, LANES), jnp.int32)], axis=1)
     padded = jnp.concatenate([padded, padded], axis=0)
     for j in range(16):
@@ -122,6 +137,8 @@
         for r in range(4):
             picks[pl.ds(8 * r + k, 1), :] = both[r : r + 1]
 
+    loads[1].wait()
+    loads[2].wait()
     for p in range(40):
         stack[pl.ds(8 * p, 8), :] = particles[:, LANES * p : LANES * p + LANES]
 
@@ -133,28 +150,6 @@
     for side, pair in ((0, 0), (1, 7)):
         index = jnp.broadcast_to(jnp.bitwise_and(faces[side : side + 1], 127), (8, LANES))
         ghost_out[side] = spread(stack[pl.ds(8 * pair, 8), :], index)
-
-    pl.semaphore_wait(barrier, 6)
-
-    def send(source, destination, number, peer):
-        copy = pltpu.make_async_remote_copy(
-            src_ref=source,
-            dst_ref=destination,
-            send_sem=send_sem.at[number],
-            recv_sem=recv_sem.at[number],
-            device_id=peer,
-            device_id_type=MESH,
-        )
-        copy.start()
-        return copy
-
-    pair_copies = [
-        send(outgoing.at[r], incoming.at[pl.ds(64 * r, 64)], r, partners[r]) for r in (3, 2, 1, 0)
-    ]
-    ghost_copies = [
-        send(ghost_out.at[0], ghost_in.at[pl.ds(8, 8)], 4, below),
-        send(ghost_out.at[1], ghost_in.at[pl.ds(0, 8)], 5, above),
-    ]
 
     filler_field = lax.broadcasted_iota(jnp.int32, (8, LANES), 0)
     filler = jnp.where(filler_field < 3, FAR, 0.0).astype(F32)
@@ -179,7 +174,13 @@
     for slot in (46, 47):
         target[pl.ds(8 * slot, 8), :] = zero
 
-    def meet(block, row, lanes, chunks, slots, term):
+    def ahead_of(ring, block, row, lanes, chunks, count, stride=1):
+        for f in range(count):
+            at = lanes + stride * f
+            for c in range(chunks):
+                ring[OWN_CHUNKS * f + c] = spread(block[pl.ds(row + 8 * c, 8), :], at)
+
+    def meet(ring, chunks, slots, term):
         sums = [zero for _ in slots]
         aims = [
             [
@@ -189,8 +190,7 @@
             for slot in slots
         ]
         for c in range(chunks):
-            rows = block[pl.ds(row + 8 * c, 8), :]
-            xs, ys, zs, us, vs, ws, mass = [spread(rows, lanes + f) for f in range(7)]
+            xs, ys, zs, us, vs, ws, mass = [ring[OWN_CHUNKS * f + c] for f in range(7)]
             for n in range(len(slots)):
                 xt, yt, zt, ut, vt, wt = aims[n]
                 dx, dy, dz = xt - xs, yt - ys, zt - zs
@@ -206,43 +206,65 @@
                 terms[place + 3] = near2 * dz
         return sums
 
-    def edge_lanes(pair_low, pair_high, stride, scale):
+    def edge_lanes(pair_low, pair_high, scale):
         return jnp.where(first_half, scale * ENTRY[pair_low], scale * ENTRY[pair_high])
 
     def own_density(walk):
         base, pairs, low, high = WALKS[walk]
         before, after = EDGES[walk]
-        block = fields.at[walk]
+        one, two, edge = rings[3 * (walk % 2) : 3 * (walk % 2) + 3]
         span = half * (32 if walk == 0 else 64)
         edge_term = 4 * (OWN_TERMS + 2 * walk * OWN_CHUNKS)
-        (start,) = meet(
-            fields.at[0], 64, edge_lanes(*before, 1, 8), OWN_CHUNKS, [base + 1], edge_term
-        )
+        ahead_of(edge, fields.at[0], 64, edge_lanes(*before, 8), OWN_CHUNKS, 7)
+        ahead_of(one, fields.at[walk], 0, span, OWN_CHUNKS, 7)
+        (start,) = meet(edge, OWN_CHUNKS, [base + 1], edge_term)
 
         def step(k, carry):
             waiting, current = carry
+            ahead_of(two, fields.at[walk], 64, span + 8 * k, OWN_CHUNKS, 7)
             for odd in (0, 1):
                 slot = base + 2 * k + odd
                 term = 4 * 3 * OWN_CHUNKS * (FIRST_STEP[walk] + 2 * k + odd)
                 behind, here, ahead = meet(
-                    block, 64 * odd, span + 8 * k, OWN_CHUNKS, [slot, slot + 1, slot + 2], term
+                    (one, two)[odd], OWN_CHUNKS, [slot, slot + 1, slot + 2], term
                 )
                 acc_density[slot] = waiting + behind
                 waiting, current = current + here, ahead
+                if odd == 0:
+                    last = k == pairs - 1
+                    lanes = jnp.where(last, edge_lanes(*after, 8), span + 8 * (k + 1))
+                    block = fields.at[jnp.where(last, 0, walk)]
+                    ahead_of(one, block, 0, lanes, OWN_CHUNKS, 7)
             return waiting, current
 
         waiting, _ = lax.fori_loop(0, pairs, step, (zero, start))
-        (end,) = meet(
-            fields.at[0],
-            0,
-            edge_lanes(*after, 1, 8),
-            OWN_CHUNKS,
-            [base + 2 * pairs],
-            edge_term + 4 * OWN_CHUNKS,
+        (end,) = meet(one, OWN_CHUNKS, [base + 2 * pairs], edge_term + 4 * OWN_CHUNKS)
+        acc_density[base + 2 * pairs] = waiting + end
+
+    own_density(1)
+
+    pl.semaphore_wait(barrier, 6)
+
+    def send(source, destination, number, peer):
+        copy = pltpu.make_async_remote_copy(
+            src_ref=source,
+            dst_ref=destination,
+            send_sem=send_sem.at[number],
+            recv_sem=recv_sem.at[number],
+            device_id=peer,
+            device_id_type=MESH,
         )
-        acc_density[base + 2 * pairs] = waiting + end
-
-    own_density(1)
+        copy.start()
+        return copy
+
+    pair_copies = [
+        send(outgoing.at[r], incoming.at[pl.ds(64 * r, 64)], r, partners[r]) for r in (3, 2, 1, 0)
+    ]
+    ghost_copies = [
+        send(ghost_out.at[0], ghost_in.at[pl.ds(8, 8)], 4, below),
+        send(ghost_out.at[1], ghost_in.at[pl.ds(0, 8)], 5, above),
+    ]
+
     own_density(2)
 
     place_in_tile = jnp.bitwise_and(lane, 63).astype(F32)
@@ -265,9 +287,12 @@
 
         row_member[pl.ds(base, 1), :] = zero[0:1]
         acc_density[base] = zero
+        one, two, _ = rings[3 * (walk % 2) : 3 * (walk % 2) + 3]
+        ahead_of(one, block, 0, 64 * half, LISTED_CHUNKS, 7)
 
         def step(k, carry):
             waiting, current = carry
+            ahead_of(two, block, 64, 64 * half + 8 * k, LISTED_CHUNKS, 7)
             for odd in (0, 1):
                 slot = base + 2 * k + odd
                 member(slot + 1, 2 * k + odd)
@@ -275,15 +300,13 @@
                     16 * (walk - 1) + 2 * k + odd
                 )
                 behind, here, ahead = meet(
-                    block,
-                    64 * odd,
-                    64 * half + 8 * k,
-                    LISTED_CHUNKS,
-                    [slot, slot + 1, slot + 2],
-                    term,
+                    (one, two)[odd], LISTED_CHUNKS, [slot, slot + 1, slot + 2], term
                 )
                 finish(slot, waiting + behind)
                 waiting, current = current + here, ahead
+                if odd == 0:
+                    after = 8 * jnp.minimum(k + 1, pairs - 1)
+                    ahead_of(one, block, 0, 64 * half + after, LISTED_CHUNKS, 7)
             return waiting, current
 
         waiting, _ = lax.fori_loop(0, pairs, step, (zero, zero))
@@ -382,15 +405,14 @@
     extra[pl.ds(48, 80), :] = jnp.zeros((80, LANES), F32)
     given[0] = jnp.transpose(extra[...])
 
-    def push(block, row, lanes, field_stride, chunks, slots, term):
+    def push(ring, chunks, slots, term):
         sums = [[zero, zero, zero] for _ in slots]
         aims = [
             [jnp.broadcast_to(rows[pl.ds(slot, 1), :], (8, LANES)) for rows in (row_a, row_b)]
             for slot in slots
         ]
         for c in range(chunks):
-            rows = block[pl.ds(row + 8 * c, 8), :]
-            a_source, b_source, gain = [spread(rows, lanes + field_stride * f) for f in range(3)]
+            a_source, b_source, gain = [ring[OWN_CHUNKS * f + c] for f in range(3)]
             for n in range(len(slots)):
                 place = term + 4 * (c * len(slots) + n)
                 star = (aims[n][0] + a_source) - terms[place]
@@ -411,9 +433,10 @@
         block = given.at[0 if walk == 0 else 1]
         field_stride = 16 if walk == 0 else 8
         edge_term = 4 * (OWN_TERMS + 2 * walk * OWN_CHUNKS)
-        (start,) = push(
-            given.at[0], 64, edge_lanes(*before, 16, 1), 16, OWN_CHUNKS, [base + 1], edge_term
-        )
+        one, two, edge = rings[3 * (walk % 2) : 3 * (walk % 2) + 3]
+        ahead_of(edge, given.at[0], 64, edge_lanes(*before, 1), OWN_CHUNKS, 3, 16)
+        ahead_of(one, block, 0, span, OWN_CHUNKS, 3, field_stride)
+        (start,) = push(edge, OWN_CHUNKS, [base + 1], edge_term)
 
         def keep(slot, sums):
             for f in range(3):
@@ -421,32 +444,23 @@
 
         def step(k, carry):
             waiting, current = carry
+            ahead_of(two, block, 64, span + k, OWN_CHUNKS, 3, field_stride)
             for odd in (0, 1):
                 slot = base + 2 * k + odd
                 term = 4 * 3 * OWN_CHUNKS * (FIRST_STEP[walk] + 2 * k + odd)
                 behind, here, ahead = push(
-                    block,
-                    64 * odd,
-                    span + k,
-                    field_stride,
-                    OWN_CHUNKS,
-                    [slot, slot + 1, slot + 2],
-                    term,
+                    (one, two)[odd], OWN_CHUNKS, [slot, slot + 1, slot + 2], term
                 )
                 keep(slot, plus(waiting, behind))
                 waiting, current = plus(current, here), ahead
+                if odd == 0:
+                    after = jnp.minimum(k + 1, pairs - 1)
+                    ahead_of(one, block, 0, span + after, OWN_CHUNKS, 3, field_stride)
             return waiting, current
 
         waiting, _ = lax.fori_loop(0, pairs, step, (zeros, start))
-        (end,) = push(
-            given.at[0],
-            0,
-            edge_lanes(*after, 16, 1),
-            16,
-            OWN_CHUNKS,
-            [base + 2 * pairs],
-            edge_term + 4 * OWN_CHUNKS,
-        )
+        ahead_of(edge, given.at[0], 0, edge_lanes(*after, 1), OWN_CHUNKS, 3, 16)
+        (end,) = push(edge, OWN_CHUNKS, [base + 2 * pairs], edge_term + 4 * OWN_CHUNKS)
         keep(base + 2 * pairs, plus(waiting, end))
 
     for walk in range(3):
@@ -476,25 +490,26 @@
 
         for f in range(3):
             acc_force[3 * base + f] = zero
+        one, two, _ = rings[3 * (walk % 2) : 3 * (walk % 2) + 3]
+        span = 24 * half + 48 * (walk - 1)
+        ahead_of(one, theirs_given, 0, span, LISTED_CHUNKS, 3, 8)
 
         def step(k, carry):
             waiting, current = carry
+            ahead_of(two, theirs_given, 64, span + k, LISTED_CHUNKS, 3, 8)
             for odd in (0, 1):
                 slot = base + 2 * k + odd
                 term = 4 * (OWN_TERMS + EDGE_TERMS) + 4 * 3 * LISTED_CHUNKS * (
                     16 * (walk - 1) + 2 * k + odd
                 )
                 behind, here, ahead = push(
-                    theirs_given,
-                    64 * odd,
-                    24 * half + (48 * (walk - 1) + k),
-                    8,
-                    LISTED_CHUNKS,
-                    [slot, slot + 1, slot + 2],
-                    term,
+                    (one, two)[odd], LISTED_CHUNKS, [slot, slot + 1, slot + 2], term
                 )
                 finish(slot, plus(waiting, behind))
                 waiting, current = plus(current, here), ahead
+                if odd == 0:
+                    after = jnp.minimum(k + 1, pairs - 1)
+                    ahead_of(one, theirs_given, 0, span + after, LISTED_CHUNKS, 3, 8)
             return waiting, current
 
         waiting, _ = lax.fori_loop(0, pairs, step, (zeros, zeros))
@@ -517,17 +532,29 @@
         copy.wait_send()
 
 
+def leave(density, accel, density_out, accel_out):
+    density_out[...] = density[...]
+    for f in range(3):
+        for p in range(40):
+            accel_out[pl.ds(f, 1), pl.ds(LANES * p, LANES)] = accel[f, pl.ds(p, 1), :]
+
+
 def local(particles, ghost_lists, pair_lists):
     vmem = pl.BlockSpec(memory_space=pltpu.VMEM)
+    hbm = pl.BlockSpec(memory_space=pltpu.HBM)
     density, accel = pl.pallas_call(
         kernel,
         out_shape=(
             jax.ShapeDtypeStruct((40, LANES), F32),
             jax.ShapeDtypeStruct((3, 40, LANES), F32),
         ),
-        in_specs=[vmem, vmem, vmem],
+        in_specs=[hbm, hbm, hbm],
         out_specs=(vmem, vmem),
         scratch_shapes=[
+            pltpu.VMEM((8, 5120), F32),
+            pltpu.VMEM((2, 64), jnp.int32),
+            pltpu.VMEM((4, 768), jnp.int32),
+            [pltpu.VMEM((7 * OWN_CHUNKS, 8, LANES), F32) for _ in range(6)],
             pltpu.VMEM((320, LANES), F32),
             pltpu.VMEM((8 * SLOTS, LANES), F32),
             pltpu.VMEM((3, 128, LANES), F32),
@@ -554,14 +581,24 @@
             pltpu.VMEM((40, LANES), F32),
             pltpu.VMEM((128, LANES), F32),
             pltpu.VMEM((128, LANES), F32),
+            pltpu.SemaphoreType.DMA((3,)),
             pltpu.SemaphoreType.DMA((10,)),
             pltpu.SemaphoreType.DMA((10,)),
         ],
         compiler_params=pltpu.CompilerParams(
             collective_id=0, has_side_effects=True, vmem_limit_bytes=44 * 1024 * 1024
         ),
-    )(particles, ghost_lists, pair_lists)
-    return density.reshape(-1), accel.reshape(3, -1)
+    )(*[pltpu.with_memory_space_constraint(a, pltpu.HBM) for a in (particles, ghost_lists, pair_lists)])
+    density, accel = pl.pallas_call(
+        leave,
+        out_shape=(
+            jax.ShapeDtypeStruct((40, LANES), F32),
+            jax.ShapeDtypeStruct((3, 40 * LANES), F32),
+        ),
+        in_specs=[vmem, vmem],
+        out_specs=(vmem, vmem),
+    )(density, accel)
+    return density.reshape(-1), accel
 
 
 def solution(mesh):

time: 36.7 us -> 28.6 us (0.78)
  Pallas kernels: 32.3 us -> 26.6 us
  local copies, waits for them, and re-layouts: 3.56 us -> 1.21 us
    pallas_call x1, Pallas kernels: 32.3 us -> 25.1 us  [local(): pl.pallas_call(kernel, out_shape=(jax.ShapeDtypeStruct((40, LANES), F32),...]
    unnamed x8 -> x4, local copies, waits for them, and re-layouts: 3.56 us -> 1.21 us
    pallas_call x0 -> x1, Pallas kernels: none -> 1.53 us  [local(): pl.pallas_call(leave, out_shape=(jax.ShapeDtypeStruct((40, LANES), F32),...]
where the time goes in v1:
time: 28.6 us; the launch traced here: 28.4 us
  Pallas kernels  26.6 us (93%)
  local copies, waits for them, and re-layouts  1.21 us (4%)
  between operations  0.65 us (2%)
    pallas_call x1, Pallas kernels, local(): pl.pallas_call(kernel, out_shape=(jax.ShapeDtypeStruct((40, LANES), F32),...  25.1 us
    pallas_call x1, Pallas kernels, local(): pl.pallas_call(leave, out_shape=(jax.ShapeDtypeStruct((40, LANES), F32),...  1.53 us
    unnamed x4, local copies, waits for them, and re-layouts  1.21 us

profile of v1, /device:TPU:56, one launch (start us, length us, event | category | flops | bytes accessed | tf_op | source)
XLA Modules:
  0.0 28.4 jit_solution(15395000675369699884)
XLA Ops:
  0.6 25.1 %shard_map.50 = (f32[40,128]{1,0:T(8,128)S(1)}, f32[3,40,128]{2,1,0:T(8,128)S(1)}) custom-call(f32[8,5120]{1,0:T(8,128)} %particles_hbm.1, s32[2,64]{1,0:T(2,128)} %ghost_hbm.1, s32[4,768]{1,0:T(4,128)} %lists_hbm.1), custom_call_target="tpu_custom_call" | custom-call | tf_op jit(solution)/shard_map/pallas_call | solution.py:545
  25.7 0.0 copy-start
  25.7 0.6 %copy-done = f32[3,40,128]{2,1,0:T(8,128)} copy-done((f32[3,40,128]{2,1,0:T(8,128)}, f32[3,40,128]{2,1,0:T(8,128)S(1)}, u32[]{:S(2)}) %copy-start) | copy-done | bytes 61464
  26.3 0.0 copy-start.1
  26.3 0.6 %copy-done.1 = f32[40,128]{1,0:T(8,128)} copy-done((f32[40,128]{1,0:T(8,128)}, f32[40,128]{1,0:T(8,128)S(1)}, u32[]{:S(2)}) %copy-start.1) | copy-done | bytes 20504
  26.9 1.5 %shard_map.51 = (f32[40,128]{1,0:T(8,128)}, f32[3,5120]{1,0:T(4,128)}) custom-call(f32[40,128]{1,0:T(8,128)} %copy-done.1, f32[3,40,128]{2,1,0:T(8,128)} %copy-done), custom_call_target="tpu_custom_call" | custom-call | tf_op jit(solution)/shard_map/pallas_call | solution.py:592
Async XLA Ops:
  25.7 0.6 %copy-start = (f32[3,40,128]{2,1,0:T(8,128)}, f32[3,40,128]{2,1,0:T(8,128)S(1)}, u32[]{:S(2)}) copy-start(f32[3,40,128]{2,1,0:T(8,128)S(1)} %get-tuple-element.7.accel) | copy-start | bytes 184324
  26.3 0.6 %copy-start.1 = (f32[40,128]{1,0:T(8,128)}, f32[40,128]{1,0:T(8,128)S(1)}, u32[]{:S(2)}) copy-start(f32[40,128]{1,0:T(8,128)S(1)} %get-tuple-element.6.density) | copy-start | bytes 61444

commit v2 on v1

v2 whole, which is shorter than its diff:
```python
import jax
import jax.numpy as jnp
from jax import lax
from jax.experimental import pallas as pl
from jax.experimental.pallas import tpu as pltpu
from jax.sharding import PartitionSpec as P

F32 = jnp.float32
REST = 8.0
FAR = -1000.0
LANES = 128
MESH = pl.DeviceIdType.MESH

WALKS = ((0, 4, 0, 4), (10, 8, 8, 16), (28, 8, 24, 32))
SLOTS = 48
OWN_CHUNKS = 8
LISTED_CHUNKS = 6
BLOCK = 8
OWN_TERMS = BLOCK * 3 * OWN_CHUNKS
LISTED_TERMS = BLOCK * 3 * LISTED_CHUNKS
TERMS = 5 * OWN_TERMS + 4 * LISTED_TERMS

ENTRIES = (0, 1, 2, 3, 4, 5, 6, 7, None, 8, 15, 16, 23, 24, 31, 32)
ENTRY = {pair: place for place, pair in enumerate(ENTRIES)}
EDGES = (((None, 3), (4, 8)), ((7, 15), (16, 24)), ((23, 31), (32, None)))


def spread(rows, lanes):
    return lax.gather(
        rows,
        lanes[:, :, None],
        lax.GatherDimensionNumbers(
            offset_dims=(),
            collapsed_slice_dims=(1,),
            start_index_map=(1,),
            operand_batching_dims=(0,),
            start_indices_batching_dims=(0,),
        ),
        slice_sizes=(1, 1),
        mode=lax.GatherScatterMode.PROMISE_IN_BOUNDS,
    )


def total(block):
    return jnp.sum(block, axis=0, keepdims=True)


def kernel(
    particles_hbm,
    ghost_hbm,
    lists_hbm,
    density_out,
    accel_out,
    particles,
    ghost_lists,
    pair_lists,
    rings,
    stack,
    target,
    fields,
    given,
    theirs,
    lists,
    lists_t,
    picks,
    outgoing,
    incoming,
    ghost_out,
    ghost_in,
    dens_out,
    dens_in,
    terms,
    acc_density,
    acc_force,
    row_density,
    row_a,
    row_b,
    row_scale,
    row_member,
    row_force,
    natural,
    extra,
    theirs_given,
    ghosts,
    load_sem,
    send_sem,
    recv_sem,
):
    loads = [
        pltpu.make_async_copy(source, destination, load_sem.at[number])
        for number, (source, destination) in enumerate(
            ((lists_hbm, pair_lists), (particles_hbm, particles), (ghost_hbm, ghost_lists))
        )
    ]
    for load in loads:
        load.start()

    grp = lax.axis_index("grp")
    dom = lax.axis_index("dom")
    n_dom = lax.axis_size("dom")

    def flipped(value, bit):
        return value + bit - 2 * bit * (lax.rem(lax.div(value, bit), 2))

    partners = (
        (grp, flipped(dom, 1)),
        (grp, flipped(dom, 4)),
        (flipped(grp, 1), dom),
        (flipped(grp, 2), dom),
    )
    below = (grp, lax.rem(dom + n_dom - 1, n_dom))
    above = (grp, lax.rem(dom + 1, n_dom))

    barrier = pltpu.get_barrier_semaphore()
    for peer in partners + (below, above):
        pl.semaphore_signal(barrier, inc=1, device_id=peer, device_id_type=MESH)

    lane = lax.broadcasted_iota(jnp.int32, (8, LANES), 1)
    first_half = lane < 64
    half = jnp.where(first_half, 0, 1)

    def pick_half(low, high):
        return jnp.where(first_half[0 : low.shape[0]], low, high)

    def swap(block):
        return pltpu.roll(block, 64, 1)

    loads[0].wait()
    padded = jnp.concatenate([pair_lists[...], jnp.zeros((4, LANES), jnp.int32)], axis=1)
    padded = jnp.concatenate([padded, padded], axis=0)
    for j in range(16):
        lists[pl.ds(8 * j, 8), :] = jnp.bitwise_and(padded[:, 48 * j : 48 * j + LANES], 63)
    for k in range(8):
        even = lists[pl.ds(16 * k, 8), :]
        odd = lists[pl.ds(16 * k + 8, 8), :]
        both = pick_half(even, swap(odd) + 64)
        for r in range(4):
            picks[pl.ds(8 * r + k, 1), :] = both[r : r + 1]

    loads[1].wait()
    loads[2].wait()
    for p in range(40):
        stack[pl.ds(8 * p, 8), :] = particles[:, LANES * p : LANES * p + LANES]

    filler_field = lax.broadcasted_iota(jnp.int32, (8, LANES), 0)
    filler = jnp.where(filler_field < 3, FAR, 0.0).astype(F32)
    is_listed = jnp.bitwise_and(lane, 63) < 48
    for r in range(4):
        for k in range(8):
            index = jnp.broadcast_to(picks[pl.ds(8 * r + k, 1), :], (8, LANES))
            picked = spread(stack[pl.ds(8 * (8 + 8 * r + k), 8), :], index)
            outgoing[r, pl.ds(8 * k, 8), :] = jnp.where(is_listed, picked, filler)
    faces = jnp.concatenate([ghost_lists[...], ghost_lists[...]], axis=1)
    for side, pair in ((0, 0), (1, 7)):
        index = jnp.broadcast_to(jnp.bitwise_and(faces[side : side + 1], 127), (8, LANES))
        ghost_out[side] = spread(stack[pl.ds(8 * pair, 8), :], index)

    fields[0] = jnp.transpose(
        jnp.concatenate(
            [filler if pair is None else stack[pl.ds(8 * pair, 8), :] for pair in ENTRIES], axis=0
        )
    )
    fields[1] = jnp.transpose(stack[pl.ds(64, 128), :])
    fields[2] = jnp.transpose(stack[pl.ds(192, 128), :])
    lists_t[...] = jnp.transpose(lists[...].astype(F32))

    zero = jnp.zeros((8, LANES), F32)
    for base, pairs, low, high in WALKS:
        for k in range(pairs):
            one = stack[pl.ds(8 * (low + k), 8), :]
            two = stack[pl.ds(8 * (high + k), 8), :]
            target[pl.ds(8 * (base + 1 + 2 * k), 8), :] = pick_half(one, swap(two))
            target[pl.ds(8 * (base + 2 + 2 * k), 8), :] = pick_half(swap(one), two)
        target[pl.ds(8 * base, 8), :] = zero
        target[pl.ds(8 * (base + 1 + 2 * pairs), 8), :] = zero
    for slot in (46, 47):
        target[pl.ds(8 * slot, 8), :] = zero

    def ahead_of(ring, block, row, lanes, chunks, count, stride=1, pace=8):
        for f in range(count):
            at = lanes + stride * f
            for c in range(chunks):
                rows = row + 8 * c if isinstance(row, int) else pl.multiple_of(row + pace * c, 8)
                ring[OWN_CHUNKS * f + c] = spread(block[pl.ds(rows, 8), :], at)

    def meet(ring, chunks, base, near_slots, term, sums):
        aims = [
            [
                jnp.broadcast_to(target[pl.ds(8 * (base + slot) + f, 1), :], (8, LANES))
                for f in range(6)
            ]
            for slot in near_slots
        ]
        for c in range(chunks):
            xs, ys, zs, us, vs, ws, mass = [ring[OWN_CHUNKS * f + c] for f in range(7)]
            for n, slot in enumerate(near_slots):
                xt, yt, zt, ut, vt, wt = aims[n]
                dx, dy, dz = xt - xs, yt - ys, zt - zs
                squared = dx * dx + dy * dy + dz * dz
                near = jnp.maximum(1.0 - squared, 0.0)
                near2 = near * near
                added = mass * (near2 * near)
                sums[slot] = sums[slot] + added if slot in sums else added
                along = (ut - us) * dx + (vt - vs) * dy + (wt - ws) * dz
                place = term + 4 * (c * len(near_slots) + n)
                terms[place] = along * lax.rsqrt(jnp.maximum(squared, 0.01))
                terms[place + 1] = near2 * dx
                terms[place + 2] = near2 * dy
                terms[place + 3] = near2 * dz
        return 4 * chunks * len(near_slots)

    def pattern(one, two):
        return jnp.where(first_half, one, two)

    def choose(b, values):
        result = values[-1]
        for number, value in reversed(list(enumerate(values[:-1]))):
            result = jnp.where(b == number, value, result)
        return result

    before = [(0, ENTRY[one], ENTRY[two]) for (one, two), _ in EDGES]
    after = [(0, ENTRY[one], ENTRY[two]) for _, (one, two) in EDGES]
    first_slots = (1, 11, 19, 29, 37)
    sources = (
        (before[0], (0, 0, 4), after[0]),
        (before[1], (1, 0, 8), (1, 4, 12)),
        ((1, 3, 11), (1, 4, 12), after[1]),
        (before[2], (2, 0, 8), (2, 4, 12)),
        ((2, 3, 11), (2, 4, 12), after[2]),
    )

    def source_of(b, i, table):
        which = 0 if i < 0 else 2 if i >= BLOCK else 1
        return [choose(b, [row[which][n] for row in table]) for n in range(len(table[0][0]))]

    def walked(b, first, stop, fill, each, done):
        sums = {}
        offset = 0
        for i in range(-1, BLOCK + 1):
            if i < BLOCK:
                fill(rings[(i + 2) % len(rings)], b, i + 1)
            else:
                fill(rings[0], jnp.minimum(b + 1, stop - 1), -1)
            near = [t for t in (i - 1, i, i + 1) if 0 <= t < BLOCK]
            offset += each(rings[(i + 1) % len(rings)], near, offset, sums)
            if i >= 1:
                done(i - 1, sums.pop(i - 1))

    def blocks(first, stop, fill, run):
        fill(rings[0], first, -1)

        def body(b, carry):
            run(b)
            return carry

        lax.fori_loop(first, stop, body, 0)

    def own_density(first, stop):
        def fill(ring, b, i):
            block, one, two = source_of(b, i, sources)
            k = i // 2 if 0 <= i < BLOCK else 0
            lanes = pattern(8 * (one + k), 8 * (two + k))
            ahead_of(ring, fields.at[block], 64 * (i % 2), lanes, OWN_CHUNKS, 7)

        def run(b):
            base = choose(b, first_slots)

            def each(ring, near, offset, sums):
                return meet(ring, OWN_CHUNKS, base, near, 4 * OWN_TERMS * b + offset, sums)

            def done(t, total_sum):
                acc_density[base + t] = total_sum

            walked(b, first, stop, fill, each, done)

        blocks(first, stop, fill, run)

    own_density(1, 3)

    pl.semaphore_wait(barrier, 6)

    def send(source, destination, number, peer):
        copy = pltpu.make_async_remote_copy(
            src_ref=source,
            dst_ref=destination,
            send_sem=send_sem.at[number],
            recv_sem=recv_sem.at[number],
            device_id=peer,
            device_id_type=MESH,
        )
        copy.start()
        return copy

    pair_copies = [
        send(outgoing.at[r], incoming.at[pl.ds(64 * r, 64)], r, partners[r]) for r in (3, 2, 1, 0)
    ]
    ghost_copies = [
        send(ghost_out.at[0], ghost_in.at[pl.ds(8, 8)], 4, below),
        send(ghost_out.at[1], ghost_in.at[pl.ds(0, 8)], 5, above),
    ]

    own_density(3, 5)
    own_density(0, 1)

    place_in_tile = jnp.bitwise_and(lane, 63).astype(F32)

    listed_sources = []
    for walk in (0, 1):
        listed_sources.append(((walk, 0, 8, 48, 0), (walk, 0, 8, 0, 8), (walk, 4, 12, 0, 8)))
        listed_sources.append(((walk, 3, 11, 64, 8), (walk, 4, 12, 0, 8), (walk, 4, 12, 48, 0)))

    def listed_density(first, stop):
        def fill(ring, b, i):
            block, one, two, row, pace = source_of(b, i, listed_sources)
            k = i // 2 if 0 <= i < BLOCK else 0
            if 0 <= i < BLOCK:
                row, pace = 64 * (i % 2), 8
            lanes = pattern(8 * (one + k), 8 * (two + k))
            ahead_of(ring, theirs.at[block], row, lanes, LISTED_CHUNKS, 7, pace=pace)

        def run(b):
            base = choose(b, first_slots[1:])

            def each(ring, near, offset, sums):
                term = 4 * (5 * OWN_TERMS + LISTED_TERMS * b) + offset
                return meet(ring, LISTED_CHUNKS, base, near, term, sums)

            def done(t, added):
                slot = base + t
                lanes = choose(b, (0, 64, 2, 66)) + 8 * t
                lanes = pattern(lanes, lanes + 1)
                found = zero
                for c in range(LISTED_CHUNKS):
                    named = spread(lists_t[pl.ds(8 * c, 8), :], lanes)
                    found = found + jnp.where(named == place_in_tile, 1.0, 0.0)
                member = total(found)
                row_member[pl.ds(slot, 1), :] = member
                row_density[pl.ds(slot, 1), :] = total(acc_density[slot] + member * added)

            walked(b, first, stop, fill, each, done)

        blocks(first, stop, fill, run)

    def to_pairs(rows, walk):
        base, pairs, low, high = WALKS[walk]
        even = rows[pl.ds(base + 1, pairs, stride=2), :]
        odd = rows[pl.ds(base + 2, pairs, stride=2), :]
        return pick_half(even, swap(odd)), pick_half(swap(even), odd)

    for copy in ghost_copies:
        copy.wait_recv()
    ghosts[...] = jnp.transpose(ghost_in[...])

    def ghost_density(pair, side):
        sums = zero
        aims = [
            jnp.broadcast_to(stack[pl.ds(8 * pair + f, 1), :], (8, LANES)) for f in range(3)
        ]
        at = jnp.zeros((8, LANES), jnp.int32) + 8 * side
        for c in range(OWN_CHUNKS):
            rows = ghosts[pl.ds(8 * c, 8), :]
            dx, dy, dz = [aims[f] - spread(rows, at + f) for f in range(3)]
            near = jnp.maximum(1.0 - (dx * dx + dy * dy + dz * dz), 0.0)
            sums = sums + spread(rows, at + 6) * (near * near * near)
        return sums

    from_lower = jnp.where(dom > 0, ghost_density(0, 0), 0.0)
    from_upper = jnp.where(dom < n_dom - 1, ghost_density(7, 1), 0.0)
    acc_density[1] = acc_density[1] + pick_half(from_lower, zero)
    acc_density[2] = acc_density[2] + pick_half(swap(from_lower), zero)
    acc_density[7] = acc_density[7] + pick_half(zero, swap(from_upper))
    acc_density[8] = acc_density[8] + pick_half(zero, from_upper)
    for slot in range(1, 9):
        row_density[pl.ds(slot, 1), :] = total(acc_density[slot])

    dens_copies = []
    for walk in (1, 2):
        for r in (2 * walk - 1, 2 * walk - 2):
            pair_copies[3 - r].wait_recv()
        theirs[walk - 1] = jnp.transpose(incoming[pl.ds(128 * (walk - 1), 128), :])
        listed_density(2 * walk - 2, 2 * walk)
        base, pairs, low, high = WALKS[walk]
        one, two = to_pairs(row_density, walk)
        natural[pl.ds(low, 8), :] = one
        natural[pl.ds(high, 8), :] = two
        for r, rows in ((2 * walk - 2, one), (2 * walk - 1, two)):
            dens_out[r] = spread(rows, picks[pl.ds(8 * r, 8), :])
        for r in (2 * walk - 1, 2 * walk - 2):
            dens_copies.append(send(dens_out.at[r], dens_in.at[r], 6 + r, partners[r]))
    one, two = to_pairs(row_density, 0)
    natural[pl.ds(0, 4), :] = one
    natural[pl.ds(4, 4), :] = two

    density_out[...] = natural[...]

    for slot in (0, 9, 10, 27, 28, 45, 46, 47):
        row_density[pl.ds(slot, 1), :] = zero[0:1] + 1.0
    for at in range(0, SLOTS, 8):
        rho = row_density[pl.ds(at, 8), :]
        sound = jnp.maximum(target[pl.ds(8 * at + 7, 8, stride=8), :], 0.5)
        inverse = 1.0 / rho
        row_a[pl.ds(at, 8), :] = sound - REST * sound * inverse
        row_b[pl.ds(at, 8), :] = 1.0 / (rho * sound)
        row_scale[pl.ds(at, 8), :] = 12.0 * inverse

    def values(rho, sound, mass):
        inverse = 1.0 / rho
        return [sound - REST * sound * inverse, 1.0 / (rho * sound), mass * inverse]

    own_values = []
    for at in range(0, 40, 8):
        own_values.append(
            values(
                natural[pl.ds(at, 8), :],
                stack[pl.ds(8 * at + 7, 8, stride=8), :],
                stack[pl.ds(8 * at + 6, 8, stride=8), :],
            )
        )
    blank = jnp.zeros((32, LANES), F32)
    given[1] = jnp.transpose(
        jnp.concatenate([own_values[n][f] for n in (1, 2, 3, 4) for f in range(3)] + [blank], axis=0)
    )
    for f in range(3):
        extra[pl.ds(16 * f, 8), :] = own_values[0][f]
        extra[pl.ds(16 * f + 8, 1), :] = zero[0:1] + (1.0 if f == 1 else 0.0)
        for place in range(9, 16):
            group, within = divmod(ENTRIES[place], 8)
            extra[pl.ds(16 * f + place, 1), :] = own_values[group][f][within : within + 1]
    extra[pl.ds(48, 80), :] = jnp.zeros((80, LANES), F32)
    given[0] = jnp.transpose(extra[...])

    def push(ring, chunks, base, near_slots, term, sums):
        aims = [
            [jnp.broadcast_to(rows[pl.ds(base + slot, 1), :], (8, LANES)) for rows in (row_a, row_b)]
            for slot in near_slots
        ]
        for c in range(chunks):
            a_source, b_source, gain = [ring[OWN_CHUNKS * f + c] for f in range(3)]
            for n, slot in enumerate(near_slots):
                place = term + 4 * (c * len(near_slots) + n)
                star = (aims[n][0] + a_source) - terms[place]
                factor = star * (1.0 / (aims[n][1] + b_source)) * gain
                added = [factor * terms[place + 1 + f] for f in range(3)]
                sums[slot] = [a + b for a, b in zip(sums[slot], added)] if slot in sums else added

        return 4 * chunks * len(near_slots)

    given_sources = []
    for number, row in enumerate(sources):
        shifted = []
        for block, one, two in row:
            if block == 0:
                shifted.append((0, one, two, 16))
            else:
                start = 48 * (block - 1)
                shifted.append((1, start + one, start + 16 + two, 8))
        given_sources.append(tuple(shifted))

    def own_force(first, stop):
        def fill(ring, b, i):
            block, one, two, stride = source_of(b, i, given_sources)
            k = i // 2 if 0 <= i < BLOCK else 0
            ahead_of(
                ring,
                given.at[block],
                64 * (i % 2),
                pattern(one + k, two + k),
                OWN_CHUNKS,
                3,
                stride,
            )

        def run(b):
            base = choose(b, first_slots)

            def each(ring, near, offset, sums):
                return push(ring, OWN_CHUNKS, base, near, 4 * OWN_TERMS * b + offset, sums)

            def done(t, sums):
                for f in range(3):
                    acc_force[3 * (base + t) + f] = sums[f]

            walked(b, first, stop, fill, each, done)

        blocks(first, stop, fill, run)

    own_force(0, 5)
    for slot in range(1, 9):
        for f in range(3):
            row_force[pl.ds(SLOTS * f + slot, 1), :] = (
                total(acc_force[3 * slot + f]) * row_scale[pl.ds(slot, 1), :]
            )

    def listed_force(first, stop):
        def fill(ring, b, i):
            block, one, two, _, _ = source_of(b, i, listed_sources)
            k = i // 2 if 0 <= i < BLOCK else 0
            ahead_of(
                ring,
                theirs_given.at[block],
                64 * (i % 2),
                pattern(one + k, 16 + two + k),
                LISTED_CHUNKS,
                3,
                8,
            )

        def run(b):
            base = choose(b, first_slots[1:])

            def each(ring, near, offset, sums):
                term = 4 * (5 * OWN_TERMS + LISTED_TERMS * b) + offset
                return push(ring, LISTED_CHUNKS, base, near, term, sums)

            def done(t, added):
                slot = base + t
                inside = row_member[pl.ds(slot, 1), :]
                scale = row_scale[pl.ds(slot, 1), :]
                for f in range(3):
                    sums = total(acc_force[3 * slot + f] + inside * added[f])
                    row_force[pl.ds(SLOTS * f + slot, 1), :] = sums * scale

            walked(b, first, stop, fill, each, done)

        blocks(first, stop, fill, run)

    for walk in (1, 2):
        partner_values = []
        for r in (2 * walk - 1, 2 * walk - 2):
            dens_copies[2 * walk - 2 + (2 * walk - 1 - r)].wait_recv()
        for r in (2 * walk - 2, 2 * walk - 1):
            partner_values += values(
                jnp.maximum(dens_in[r], 0.01),
                jnp.maximum(incoming[pl.ds(64 * r + 7, 8, stride=8), :], 0.5),
                incoming[pl.ds(64 * r + 6, 8, stride=8), :],
            )
        rest = [jnp.zeros((80, LANES), F32)]
        theirs_given[walk - 1] = jnp.transpose(jnp.concatenate(partner_values + rest, axis=0))
        listed_force(2 * walk - 2, 2 * walk)
    for f in range(3):
        for walk in range(3):
            base, pairs, low, high = WALKS[walk]
            one, two = to_pairs(row_force.at[pl.ds(SLOTS * f, SLOTS)], walk)
            for k in range(pairs):
                accel_out[pl.ds(f, 1), pl.ds(LANES * (low + k), LANES)] = one[k : k + 1]
                accel_out[pl.ds(f, 1), pl.ds(LANES * (high + k), LANES)] = two[k : k + 1]
    for copy in pair_copies + ghost_copies + dens_copies:
        copy.wait_send()


def leave(density, accel, density_out, accel_out, sem):
    copies = [
        pltpu.make_async_copy(accel, accel_out, sem.at[0]),
        pltpu.make_async_copy(density, density_out, sem.at[1]),
    ]
    for copy in copies:
        copy.start()
    for copy in copies:
        copy.wait()


def local(particles, ghost_lists, pair_lists):
    vmem = pl.BlockSpec(memory_space=pltpu.VMEM)
    hbm = pl.BlockSpec(memory_space=pltpu.HBM)
    density, accel = pl.pallas_call(
        kernel,
        out_shape=(
            pltpu.VMEM((40, LANES), F32),
            pltpu.VMEM((3, 40 * LANES), F32),
        ),
        in_specs=[hbm, hbm, hbm],
        out_specs=(vmem, vmem),
        scratch_shapes=[
            pltpu.VMEM((8, 5120), F32),
            pltpu.VMEM((2, 64), jnp.int32),
            pltpu.VMEM((4, 768), jnp.int32),
            [pltpu.VMEM((7 * OWN_CHUNKS, 8, LANES), F32) for _ in range(5)],
            pltpu.VMEM((320, LANES), F32),
            pltpu.VMEM((8 * SLOTS, LANES), F32),
            pltpu.VMEM((3, 128, LANES), F32),
            pltpu.VMEM((2, 128, LANES), F32),
            pltpu.VMEM((2, 128, LANES), F32),
            pltpu.VMEM((128, LANES), jnp.int32),
            pltpu.VMEM((128, LANES), F32),
            pltpu.VMEM((32, LANES), jnp.int32),
            pltpu.VMEM((4, 64, LANES), F32),
            pltpu.VMEM((256, LANES), F32),
            pltpu.VMEM((2, 8, LANES), F32),
            pltpu.VMEM((128, LANES), F32),
            pltpu.VMEM((4, 8, LANES), F32),
            pltpu.VMEM((4, 8, LANES), F32),
            pltpu.VMEM((4 * TERMS, 8, LANES), F32),
            pltpu.VMEM((SLOTS, 8, LANES), F32),
            pltpu.VMEM((3 * SLOTS, 8, LANES), F32),
            pltpu.VMEM((SLOTS, LANES), F32),
            pltpu.VMEM((SLOTS, LANES), F32),
            pltpu.VMEM((SLOTS, LANES), F32),
            pltpu.VMEM((SLOTS, LANES), F32),
            pltpu.VMEM((SLOTS, LANES), F32),
            pltpu.VMEM((3 * SLOTS, LANES), F32),
            pltpu.VMEM((40, LANES), F32),
            pltpu.VMEM((128, LANES), F32),
            pltpu.VMEM((2, 128, LANES), F32),
            pltpu.VMEM((128, LANES), F32),
            pltpu.SemaphoreType.DMA((3,)),
            pltpu.SemaphoreType.DMA((10,)),
            pltpu.SemaphoreType.DMA((10,)),
        ],
        compiler_params=pltpu.CompilerParams(
            collective_id=0, has_side_effects=True, vmem_limit_bytes=44 * 1024 * 1024
        ),
    )(*[pltpu.with_memory_space_constraint(a, pltpu.HBM) for a in (particles, ghost_lists, pair_lists)])
    density, accel = pl.pallas_call(
        leave,
        out_shape=(
            jax.ShapeDtypeStruct((40, LANES), F32),
            jax.ShapeDtypeStruct((3, 40 * LANES), F32),
        ),
        in_specs=[vmem, vmem],
        out_specs=(hbm, hbm),
        scratch_shapes=[pltpu.SemaphoreType.DMA((2,))],
    )(*[pltpu.with_memory_space_constraint(a, pltpu.VMEM) for a in (density, accel)])
    return density.reshape(-1), accel


def solution(mesh):
    in_specs = (P(None, ("grp", "dom")), P(None, ("grp", "dom")), P(None, ("grp", "dom")))
    out_specs = (P(("grp", "dom")), P(None, ("grp", "dom")))
    return jax.shard_map(local, mesh=mesh, in_specs=in_specs, out_specs=out_specs, check_vma=False)
```

time: 28.6 us -> 26.8 us (0.937)
  local copies, waits for them, and re-layouts: 1.21 us -> 0 us
  Pallas kernels: 26.6 us -> 25.9 us
    unnamed x4 -> x0, local copies, waits for them, and re-layouts: 1.21 us -> none
    pallas_call x1, Pallas kernels: 1.53 us -> 0.66 us  [local(): pl.pallas_call(leave, out_shape=(jax.ShapeDtypeStruct((40, LANES), F32),...]
where the time goes in v2:
time: 26.8 us; the launch traced here: 26.5 us
  Pallas kernels  25.9 us (97%)
  between operations  0.64 us (2%)
    pallas_call x1, Pallas kernels, local(): pl.pallas_call(kernel, out_shape=(pltpu.VMEM((40, LANES), F32), pltpu.VME...  25.2 us
    pallas_call x1, Pallas kernels, local(): pl.pallas_call(leave, out_shape=(jax.ShapeDtypeStruct((40, LANES), F32),...  0.66 us

profile of v2, /device:TPU:56, one launch (start us, length us, event | category | flops | bytes accessed | tf_op | source)
XLA Modules:
  0.0 26.5 jit_solution(3814650689798859754)
XLA Ops:
  0.6 25.2 %shard_map.50 = (f32[40,128]{1,0:T(8,128)S(1)}, f32[3,5120]{1,0:T(4,128)S(1)}) custom-call(f32[8,5120]{1,0:T(8,128)} %particles_hbm.1, s32[2,64]{1,0:T(2,128)} %ghost_hbm.1, s32[4,768]{1,0:T(4,128)} %lists_hbm.1), custom_call_target="tpu_custom_call" | custom-call | tf_op jit(solution)/shard_map/pallas_call | solution.py:565
  25.8 0.7 %shard_map.51 = (f32[40,128]{1,0:T(8,128)}, f32[3,5120]{1,0:T(4,128)}) custom-call(f32[40,128]{1,0:T(8,128)S(1)} %get-tuple-element.6.density, f32[3,5120]{1,0:T(4,128)S(1)} %get-tuple-element.7.accel), custom_call_target="tpu_custom_call" | custom-call | tf_op jit(solution)/shard_map/pallas_call | solution.py:613

commit v3 on v2

--- a/solution.py
+++ b/solution.py
@@ -161,8 +161,6 @@
         )
     )
     fields[1] = jnp.transpose(stack[pl.ds(64, 128), :])
-    fields[2] = jnp.transpose(stack[pl.ds(192, 128), :])
-    lists_t[...] = jnp.transpose(lists[...].astype(F32))
 
     zero = jnp.zeros((8, LANES), F32)
     for base, pairs, low, high in WALKS:
@@ -275,7 +273,7 @@
 
         blocks(first, stop, fill, run)
 
-    own_density(1, 3)
+    own_density(1, 2)
 
     pl.semaphore_wait(barrier, 6)
 
@@ -299,8 +297,10 @@
         send(ghost_out.at[1], ghost_in.at[pl.ds(0, 8)], 5, above),
     ]
 
-    own_density(3, 5)
-    own_density(0, 1)
+    fields[2] = jnp.transpose(stack[pl.ds(192, 128), :])
+    lists_t[...] = jnp.transpose(lists[...].astype(F32))
+
+    own_density(2, 5)
 
     place_in_tile = jnp.bitwise_and(lane, 63).astype(F32)
 
@@ -346,32 +346,6 @@
         even = rows[pl.ds(base + 1, pairs, stride=2), :]
         odd = rows[pl.ds(base + 2, pairs, stride=2), :]
         return pick_half(even, swap(odd)), pick_half(swap(even), odd)
-
-    for copy in ghost_copies:
-        copy.wait_recv()
-    ghosts[...] = jnp.transpose(ghost_in[...])
-
-    def ghost_density(pair, side):
-        sums = zero
-        aims = [
-            jnp.broadcast_to(stack[pl.ds(8 * pair + f, 1), :], (8, LANES)) for f in range(3)
-        ]
-        at = jnp.zeros((8, LANES), jnp.int32) + 8 * side
-        for c in range(OWN_CHUNKS):
-            rows = ghosts[pl.ds(8 * c, 8), :]
-            dx, dy, dz = [aims[f] - spread(rows, at + f) for f in range(3)]
-            near = jnp.maximum(1.0 - (dx * dx + dy * dy + dz * dz), 0.0)
-            sums = sums + spread(rows, at + 6) * (near * near * near)
-        return sums
-
-    from_lower = jnp.where(dom > 0, ghost_density(0, 0), 0.0)
-    from_upper = jnp.where(dom < n_dom - 1, ghost_density(7, 1), 0.0)
-    acc_density[1] = acc_density[1] + pick_half(from_lower, zero)
-    acc_density[2] = acc_density[2] + pick_half(swap(from_lower), zero)
-    acc_density[7] = acc_density[7] + pick_half(zero, swap(from_upper))
-    acc_density[8] = acc_density[8] + pick_half(zero, from_upper)
-    for slot in range(1, 9):
-        row_density[pl.ds(slot, 1), :] = total(acc_density[slot])
 
     dens_copies = []
     for walk in (1, 2):
@@ -387,6 +361,33 @@
             dens_out[r] = spread(rows, picks[pl.ds(8 * r, 8), :])
         for r in (2 * walk - 1, 2 * walk - 2):
             dens_copies.append(send(dens_out.at[r], dens_in.at[r], 6 + r, partners[r]))
+    own_density(0, 1)
+    for copy in ghost_copies:
+        copy.wait_recv()
+    ghosts[...] = jnp.transpose(ghost_in[...])
+
+    def ghost_density(pair, side):
+        sums = zero
+        aims = [
+            jnp.broadcast_to(stack[pl.ds(8 * pair + f, 1), :], (8, LANES)) for f in range(3)
+        ]
+        at = jnp.zeros((8, LANES), jnp.int32) + 8 * side
+        for c in range(OWN_CHUNKS):
+            rows = ghosts[pl.ds(8 * c, 8), :]
+            dx, dy, dz = [aims[f] - spread(rows, at + f) for f in range(3)]
+            near = jnp.maximum(1.0 - (dx * dx + dy * dy + dz * dz), 0.0)
+            sums = sums + spread(rows, at + 6) * (near * near * near)
+        return sums
+
+    from_lower = jnp.where(dom > 0, ghost_density(0, 0), 0.0)
+    from_upper = jnp.where(dom < n_dom - 1, ghost_density(7, 1), 0.0)
+    acc_density[1] = acc_density[1] + pick_half(from_lower, zero)
+    acc_density[2] = acc_density[2] + pick_half(swap(from_lower), zero)
+    acc_density[7] = acc_density[7] + pick_half(zero, swap(from_upper))
+    acc_density[8] = acc_density[8] + pick_half(zero, from_upper)
+    for slot in range(1, 9):
+        row_density[pl.ds(slot, 1), :] = total(acc_density[slot])
+
     one, two = to_pairs(row_density, 0)
     natural[pl.ds(0, 4), :] = one
     natural[pl.ds(4, 4), :] = two

time: 26.8 us -> 26.7 us (level)
  no operation moved by 1% of the time
where the time goes in v3:
time: 26.7 us; the launch traced here: 26.4 us
  Pallas kernels  25.8 us (97%)
  between operations  0.64 us (2%)
    pallas_call x1, Pallas kernels, local(): pl.pallas_call(kernel, out_shape=(pltpu.VMEM((40, LANES), F32), pltpu.VME...  25.2 us
    pallas_call x1, Pallas kernels, local(): pl.pallas_call(leave, out_shape=(jax.ShapeDtypeStruct((40, LANES), F32),...  0.66 us

profile of v3, /device:TPU:56, one launch (start us, length us, event | category | flops | bytes accessed | tf_op | source)
XLA Modules:
  0.0 26.4 jit_solution(11252681636709273664)
XLA Ops:
  0.6 25.2 %shard_map.50 = (f32[40,128]{1,0:T(8,128)S(1)}, f32[3,5120]{1,0:T(4,128)S(1)}) custom-call(f32[8,5120]{1,0:T(8,128)} %particles_hbm.1, s32[2,64]{1,0:T(2,128)} %ghost_hbm.1, s32[4,768]{1,0:T(4,128)} %lists_hbm.1), custom_call_target="tpu_custom_call" | custom-call | tf_op jit(solution)/shard_map/pallas_call | solution.py:566
  25.8 0.7 %shard_map.51 = (f32[40,128]{1,0:T(8,128)}, f32[3,5120]{1,0:T(4,128)}) custom-call(f32[40,128]{1,0:T(8,128)S(1)} %get-tuple-element.6.density, f32[3,5120]{1,0:T(4,128)S(1)} %get-tuple-element.7.accel), custom_call_target="tpu_custom_call" | custom-call | tf_op jit(solution)/shard_map/pallas_call | solution.py:614

commit v4 on v3

--- a/solution.py
+++ b/solution.py
@@ -55,6 +55,8 @@
     ghost_lists,
     pair_lists,
     rings,
+    wide_rings,
+    select,
     stack,
     target,
     fields,
@@ -144,23 +146,49 @@
 
     filler_field = lax.broadcasted_iota(jnp.int32, (8, LANES), 0)
     filler = jnp.where(filler_field < 3, FAR, 0.0).astype(F32)
-    is_listed = jnp.bitwise_and(lane, 63) < 48
     for r in range(4):
         for k in range(8):
             index = jnp.broadcast_to(picks[pl.ds(8 * r + k, 1), :], (8, LANES))
             picked = spread(stack[pl.ds(8 * (8 + 8 * r + k), 8), :], index)
-            outgoing[r, pl.ds(8 * k, 8), :] = jnp.where(is_listed, picked, filler)
+            outgoing[r, pl.ds(8 * k, 8), :] = picked
     faces = jnp.concatenate([ghost_lists[...], ghost_lists[...]], axis=1)
     for side, pair in ((0, 0), (1, 7)):
         index = jnp.broadcast_to(jnp.bitwise_and(faces[side : side + 1], 127), (8, LANES))
         ghost_out[side] = spread(stack[pl.ds(8 * pair, 8), :], index)
 
-    fields[0] = jnp.transpose(
-        jnp.concatenate(
-            [filler if pair is None else stack[pl.ds(8 * pair, 8), :] for pair in ENTRIES], axis=0
-        )
-    )
-    fields[1] = jnp.transpose(stack[pl.ds(64, 128), :])
+    wide_row = lax.broadcasted_iota(jnp.int32, (128, 7 * LANES), 0)
+    wide_lane = lax.broadcasted_iota(jnp.int32, (128, 7 * LANES), 1)
+    for parity in (0, 1):
+        wanted = 32 * parity + jnp.where(jnp.bitwise_and(wide_lane, 127) < 64, 0, 64) + wide_lane // LANES
+        gap = wide_row - wanted
+        chosen = jnp.where((gap == 0) | (gap == 8) | (gap == 16), 1.0, 0.0)
+        select[parity] = chosen.astype(jnp.bfloat16)
+
+    def pieces(rows):
+        result = []
+        for _ in range(3):
+            piece = rows.astype(jnp.bfloat16).astype(F32)
+            result.append(piece)
+            rows = rows - piece
+        return result + [jnp.zeros((8, LANES), F32)]
+
+    def standing(blocks_of_rows):
+        rows = [piece for rows in blocks_of_rows for piece in pieces(rows)]
+        return jnp.transpose(jnp.concatenate(rows, axis=0)).astype(jnp.bfloat16)
+
+    def pair_rows(pair):
+        return filler if pair is None else stack[pl.ds(8 * pair, 8), :]
+
+    def stand(walk):
+        _, pairs, low, high = WALKS[walk]
+        for number in range(pairs // 2):
+            four = (low + 2 * number, low + 2 * number + 1, high + 2 * number, high + 2 * number + 1)
+            fields[(0, 2, 6)[walk] + number] = standing([pair_rows(pair) for pair in four])
+        (low_before, high_before), (low_after, high_after) = EDGES[walk]
+        four = (low_after, low_before, high_after, high_before)
+        fields[10 + walk] = standing([pair_rows(pair) for pair in four])
+
+    stand(1)
 
     zero = jnp.zeros((8, LANES), F32)
     for base, pairs, low, high in WALKS:
@@ -181,7 +209,54 @@
                 rows = row + 8 * c if isinstance(row, int) else pl.multiple_of(row + pace * c, 8)
                 ring[OWN_CHUNKS * f + c] = spread(block[pl.ds(rows, 8), :], at)
 
-    def meet(ring, chunks, base, near_slots, term, sums):
+    def widen(ring, block, parity, first, count):
+        rows = block[pl.ds(first, count), :]
+        for start in range(0, 7, 2):
+            width = min(2, 7 - start)
+            wide = jnp.dot(
+                rows,
+                select[parity, :, LANES * start : LANES * (start + width)],
+                preferred_element_type=F32,
+            )
+            for f in range(width):
+                for c in range(count // 8):
+                    ring[16 * (start + f) + first // 8 + c] = wide[
+                        8 * c : 8 * c + 8, LANES * f : LANES * f + LANES
+                    ]
+
+    def widen_unit(ring, block, unit):
+        if unit == -1:
+            widen(ring, block, 1, 64, 64)
+        elif unit == 4:
+            widen(ring, block, 0, 0, 64)
+        else:
+            widen(ring, block, unit % 2, 0, 128)
+
+    def walked_wide(b, stop, fill, each, done):
+        sums = {}
+        offset = 0
+        for number, unit in enumerate(range(-1, 5)):
+            if unit < 4:
+                fill(wide_rings[(number + 1) % 3], b, unit + 1)
+            else:
+                fill(wide_rings[0], jnp.minimum(b + 1, stop - 1), -1)
+            steps = {-1: [(-1, 8)], 4: [(8, 0)]}.get(unit, [(2 * unit, 0), (2 * unit + 1, 8)])
+            for i, start in steps:
+                near = [t for t in (i - 1, i, i + 1) if 0 <= t < BLOCK]
+                offset += each(wide_rings[number % 3], near, offset, sums, start)
+                if i >= 1:
+                    done(i - 1, sums.pop(i - 1))
+
+    def wide_blocks(first, stop, fill, run):
+        fill(wide_rings[0], first, -1)
+
+        def body(b, carry):
+            run(b)
+            return carry
+
+        lax.fori_loop(first, stop, body, 0)
+
+    def meet(ring, chunks, base, near_slots, term, sums, start):
         aims = [
             [
                 jnp.broadcast_to(target[pl.ds(8 * (base + slot) + f, 1), :], (8, LANES))
@@ -190,7 +265,7 @@
             for slot in near_slots
         ]
         for c in range(chunks):
-            xs, ys, zs, us, vs, ws, mass = [ring[OWN_CHUNKS * f + c] for f in range(7)]
+            xs, ys, zs, us, vs, ws, mass = [ring[16 * f + start + c] for f in range(7)]
             for n, slot in enumerate(near_slots):
                 xt, yt, zt, ut, vt, wt = aims[n]
                 dx, dy, dz = xt - xs, yt - ys, zt - zs
@@ -254,24 +329,23 @@
         lax.fori_loop(first, stop, body, 0)
 
     def own_density(first, stop):
-        def fill(ring, b, i):
-            block, one, two = source_of(b, i, sources)
-            k = i // 2 if 0 <= i < BLOCK else 0
-            lanes = pattern(8 * (one + k), 8 * (two + k))
-            ahead_of(ring, fields.at[block], 64 * (i % 2), lanes, OWN_CHUNKS, 7)
+        def fill(ring, b, unit):
+            which = {-1: (10, 11, 3, 12, 7), 4: (10, 4, 11, 8, 12)}.get(unit, (0, 2, 4, 6, 8))
+            number = choose(b, which) + (unit // 2 if 0 <= unit < 4 else 0)
+            widen_unit(ring, fields.at[number], unit)
 
         def run(b):
             base = choose(b, first_slots)
 
-            def each(ring, near, offset, sums):
-                return meet(ring, OWN_CHUNKS, base, near, 4 * OWN_TERMS * b + offset, sums)
+            def each(ring, near, offset, sums, start):
+                return meet(ring, OWN_CHUNKS, base, near, 4 * OWN_TERMS * b + offset, sums, start)
 
             def done(t, total_sum):
                 acc_density[base + t] = total_sum
 
-            walked(b, first, stop, fill, each, done)
-
-        blocks(first, stop, fill, run)
+            walked_wide(b, stop, fill, each, done)
+
+        wide_blocks(first, stop, fill, run)
 
     own_density(1, 2)
 
@@ -297,7 +371,8 @@
         send(ghost_out.at[1], ghost_in.at[pl.ds(0, 8)], 5, above),
     ]
 
-    fields[2] = jnp.transpose(stack[pl.ds(192, 128), :])
+    stand(2)
+    stand(0)
     lists_t[...] = jnp.transpose(lists[...].astype(F32))
 
     own_density(2, 5)
@@ -310,20 +385,17 @@
         listed_sources.append(((walk, 3, 11, 64, 8), (walk, 4, 12, 0, 8), (walk, 4, 12, 48, 0)))
 
     def listed_density(first, stop):
-        def fill(ring, b, i):
-            block, one, two, row, pace = source_of(b, i, listed_sources)
-            k = i // 2 if 0 <= i < BLOCK else 0
-            if 0 <= i < BLOCK:
-                row, pace = 64 * (i % 2), 8
-            lanes = pattern(8 * (one + k), 8 * (two + k))
-            ahead_of(ring, theirs.at[block], row, lanes, LISTED_CHUNKS, 7, pace=pace)
+        def fill(ring, b, unit):
+            which = {-1: (8, 1, 8, 5), 4: (2, 8, 6, 8)}.get(unit, (0, 2, 4, 6))
+            number = choose(b, which) + (unit // 2 if 0 <= unit < 4 else 0)
+            widen_unit(ring, theirs.at[number], unit)
 
         def run(b):
             base = choose(b, first_slots[1:])
 
-            def each(ring, near, offset, sums):
+            def each(ring, near, offset, sums, start):
                 term = 4 * (5 * OWN_TERMS + LISTED_TERMS * b) + offset
-                return meet(ring, LISTED_CHUNKS, base, near, term, sums)
+                return meet(ring, LISTED_CHUNKS, base, near, term, sums, start)
 
             def done(t, added):
                 slot = base + t
@@ -337,9 +409,9 @@
                 row_member[pl.ds(slot, 1), :] = member
                 row_density[pl.ds(slot, 1), :] = total(acc_density[slot] + member * added)
 
-            walked(b, first, stop, fill, each, done)
-
-        blocks(first, stop, fill, run)
+            walked_wide(b, stop, fill, each, done)
+
+        wide_blocks(first, stop, fill, run)
 
     def to_pairs(rows, walk):
         base, pairs, low, high = WALKS[walk]
@@ -347,11 +419,14 @@
         odd = rows[pl.ds(base + 2, pairs, stride=2), :]
         return pick_half(even, swap(odd)), pick_half(swap(even), odd)
 
+    theirs[8] = standing([filler] * 4)
     dens_copies = []
     for walk in (1, 2):
         for r in (2 * walk - 1, 2 * walk - 2):
             pair_copies[3 - r].wait_recv()
-        theirs[walk - 1] = jnp.transpose(incoming[pl.ds(128 * (walk - 1), 128), :])
+        for number in range(4):
+            starts = [128 * (walk - 1) + at + 16 * number for at in (0, 8, 64, 72)]
+            theirs[4 * (walk - 1) + number] = standing([incoming[pl.ds(at, 8), :] for at in starts])
         listed_density(2 * walk - 2, 2 * walk)
         base, pairs, low, high = WALKS[walk]
         one, two = to_pairs(row_density, walk)
@@ -575,12 +650,14 @@
             pltpu.VMEM((8, 5120), F32),
             pltpu.VMEM((2, 64), jnp.int32),
             pltpu.VMEM((4, 768), jnp.int32),
-            [pltpu.VMEM((7 * OWN_CHUNKS, 8, LANES), F32) for _ in range(5)],
+            [pltpu.VMEM((3 * OWN_CHUNKS, 8, LANES), F32) for _ in range(5)],
+            [pltpu.VMEM((7 * 16, 8, LANES), F32) for _ in range(3)],
+            pltpu.VMEM((2, 128, 7 * LANES), jnp.bfloat16),
             pltpu.VMEM((320, LANES), F32),
             pltpu.VMEM((8 * SLOTS, LANES), F32),
-            pltpu.VMEM((3, 128, LANES), F32),
+            pltpu.VMEM((13, 128, LANES), jnp.bfloat16),
             pltpu.VMEM((2, 128, LANES), F32),
-            pltpu.VMEM((2, 128, LANES), F32),
+            pltpu.VMEM((9, 128, LANES), jnp.bfloat16),
             pltpu.VMEM((128, LANES), jnp.int32),
             pltpu.VMEM((128, LANES), F32),
             pltpu.VMEM((32, LANES), jnp.int32),

time: 26.7 us -> 26.3 us (0.985)
  Pallas kernels: 25.8 us -> 25.4 us
    pallas_call x1, Pallas kernels: 25.2 us -> 24.7 us  [local(): pl.pallas_call(kernel, out_shape=(pltpu.VMEM((40, LANES), F32), pltpu.VME...]
where the time goes in v4:
time: 26.3 us; the launch traced here: 26 us
  Pallas kernels  25.4 us (97%)
  between operations  0.64 us (2%)
    pallas_call x1, Pallas kernels, local(): pl.pallas_call(kernel, out_shape=(pltpu.VMEM((40, LANES), F32), pltpu.VME...  24.7 us
    pallas_call x1, Pallas kernels, local(): pl.pallas_call(leave, out_shape=(jax.ShapeDtypeStruct((40, LANES), F32),...  0.66 us

profile of v4, /device:TPU:56, one launch (start us, length us, event | category | flops | bytes accessed | tf_op | source)
XLA Modules:
  0.0 26.0 jit_solution(10635506852637659009)
XLA Ops:
  0.6 24.7 %shard_map.50 = (f32[40,128]{1,0:T(8,128)S(1)}, f32[3,5120]{1,0:T(4,128)S(1)}) custom-call(f32[8,5120]{1,0:T(8,128)} %particles_hbm.1, s32[2,64]{1,0:T(2,128)} %ghost_hbm.1, s32[4,768]{1,0:T(4,128)} %lists_hbm.1), custom_call_target="tpu_custom_call" | custom-call | tf_op jit(solution)/shard_map/pallas_call | solution.py:641
  25.4 0.7 %shard_map.51 = (f32[40,128]{1,0:T(8,128)}, f32[3,5120]{1,0:T(4,128)}) custom-call(f32[40,128]{1,0:T(8,128)S(1)} %get-tuple-element.6.density, f32[3,5120]{1,0:T(4,128)S(1)} %get-tuple-element.7.accel), custom_call_target="tpu_custom_call" | custom-call | tf_op jit(solution)/shard_map/pallas_call | solution.py:691
